TPU v7x, 512 devices: a whole 4x4x16 slice. The times are simulated.
512 devices in a mesh: cuts: 2 (over y_lo), dp: 16 (over z), row: 4 (over y_hi, core), col: 4 (over x).
Axes of the slice: x: 4, y: 4 (y_hi: 2, y_lo: 2; y = y_hi * 2 + y_lo), z: 16, core: 2. Of those that a mesh axis runs over, the one named last changes fastest.
Arguments:
- tokens: bfloat16 [32768, 4096], P(('cuts', 'dp'), 'row'), may hold values from -6 to 6
- cotangent: bfloat16 [32768, 4096], P(('cuts', 'dp'), 'col'), may hold values from -0.03125 to 0.03125
- norm_gain: float32 [4096], P('row'), may hold values from 0.5 to 6
- row_prev: float32 [4, 1024], P('row', 'dp'), may hold values from 0.02 to 0.5
- col_prev: float32 [4096], P('col'), may hold values from 0.002 to 0.05
Outputs:
- update: float32 [4, 1024, 4096], P('row', 'dp', 'col')
- row_moment: float32 [4, 1024], P('row', 'dp')
- col_moment: float32 [4096], P('col')
All inputs are finite; a program needn't handle non-finite values.
Results may differ from a plain program's by a relative error of at most 0.0004.
Values sent between devices are 32-bit elements; how exact they have to be, the bound alone decides.
A program may use at most 64 MiB of HBM per device.

v0:
```python
import jax
import jax.numpy as jnp
from jax import lax
from jax.sharding import PartitionSpec as P

D = 4096
F = 4096
decay_rate = 0.975
epsilon_one = 1e-30
clip_level = 1.0


def gradient_rows(inputs, cotangent, gains):
    product = lax.dot_general(
        inputs, cotangent, (((0,), (0,)), ((), ())), preferred_element_type=jnp.float32
    )
    return product * gains[:, None]


def adafactor_step(gradient, rows_prev, cols_prev, down_columns, all_total):
    squares = gradient * gradient
    row_sum = lax.psum(jnp.sum(squares, axis=1), "col")
    col_sum = down_columns(jnp.sum(squares, axis=0))
    row_moment = decay_rate * rows_prev + (1.0 - decay_rate) * (row_sum / F + epsilon_one)
    col_moment = decay_rate * cols_prev + (1.0 - decay_rate) * (col_sum / D + epsilon_one)
    factor = row_moment[:, None] * col_moment[None, :]
    raw_update = gradient / jnp.sqrt(factor)
    total_squares = all_total(jnp.sum(raw_update * raw_update))
    clip_scale = jnp.maximum(1.0, jnp.sqrt(total_squares / (D * F)) / clip_level)
    return (raw_update / clip_scale, row_moment, col_moment)


def body(tokens, cotangent, norm_gain, row_prev, col_prev):
    slice_part = lax.psum_scatter(
        gradient_rows(tokens, cotangent, norm_gain), "dp", scatter_dimension=0, tiled=True
    )
    gradient = lax.psum(slice_part, "cuts")
    update, row_moment, col_moment = adafactor_step(
        gradient,
        row_prev[0],
        col_prev,
        lambda values: lax.psum(values, ("dp", "row")),
        lambda values: lax.psum(values, ("dp", "row", "col")),
    )
    return (update[None], row_moment[None], col_moment)


def solution(mesh):
    return jax.shard_map(
        body,
        mesh=mesh,
        in_specs=(
            P(("cuts", "dp"), "row"),
            P(("cuts", "dp"), "col"),
            P("row"),
            P("row", "dp"),
            P("col"),
        ),
        out_specs=(P("row", "dp", "col"), P("row", "dp"), P("col")),
        check_vma=False,
    )
```

profile of v0, /device:TPU:2, one launch (start us, length us, event | category | flops | bytes accessed | tf_op | source)
XLA Modules:
  0.0 946.8 jit_solution(15512773143829418762)
XLA Ops:
  7.2 0.0 copy-start
  7.2 0.0 reduce-scatter.2.cloned.1.call-start
  7.2 1.5 copy-done
  8.8 5.9 convolution_multiply_fusion
  14.7 0.0 copy-start.4
  14.7 0.0 copy-start.2
  14.7 0.0 reduce-scatter.2.cloned.1.call-update
  14.7 0.0 all-reduce.2.cloned.1.call-start
  14.7 84.2 %reduce-scatter.2.cloned.1.call-done = f32[64,1024]{1,0:T(8,128)} async-done(((f32[1024,1024]{1,0:T(8,128)}), f32[64,1024]{1,0:T(8,128)}) %reduce-scatter.2.cloned.1.call-update) | async-done | bytes 262160 | tf_op jit(solution)/shard_map/reduce_scatter | solution.py:34
  99.0 0.0 all-reduce.2.cloned.1.call-update
  99.0 45.7 %all-reduce.2.cloned.1.call-done = f32[64,1024]{1,0:T(8,128)} async-done(((f32[64,1024]{1,0:T(8,128)}), f32[64,1024]{1,0:T(8,128)}) %all-reduce.2.cloned.1.call-update) | async-done | bytes 262160 | tf_op jit(solution)/shard_map/psum | solution.py:37
  144.7 1.1 multiply_reduce_fusion.2
  145.8 8.6 psum.29
  154.4 132.2 %psum.30 = f32[1024]{0:T(1024)S(1)} all-reduce(f32[1024]{0:T(1024)S(1)} %get-tuple-element.4), channel_id=1, replica_groups=mesh['cuts'=2,'dp'=16,'row'=4,'col'=4] {'dp','row'}, use_global_device_ids=true, to_apply=%region_5.0 | all-reduce | flops 1024 | bytes 8192 | tf_op jit(solution)/shard_map/psum | solution.py:42
  286.6 0.0 copy-done.4
  286.6 0.0 copy-done.2
  286.6 0.0 copy-start.3
  286.7 0.0 copy-start.1
  286.7 1.7 multiply_reduce_fusion
  288.4 649.1 %psum.31 = f32[]{:T(128)} all-reduce(f32[]{:T(128)} %multiply_reduce_fusion), channel_id=1, replica_groups=mesh['cuts'=2,'dp'=16,'row'=4,'col'=4] {'dp','row','col'}, use_global_device_ids=true, to_apply=%region_7.0 | all-reduce | flops 1 | bytes 8 | tf_op jit(solution)/shard_map/psum | solution.py:43
  938.2 1.8 divide_bitcast_fusion
  939.9 0.0 copy-done.3
  939.9 0.0 copy-done.1
  (2 shorter events, 0.0 us)
Async XLA Ops:
  7.2 1.6 copy-start
  7.2 91.8 %reduce-scatter.2.cloned.1.call-start = ((), (), s32[]{:S(2)}) async-start(), calls=%async_computation.1 | async-start | bytes 4456448 | tf_op jit(solution)/shard_map/reduce_scatter | solution.py:34
  14.7 272.0 %copy-start.4 = (f32[1,64]{1,0:T(1,128)S(1)}, f32[1,64]{1,0:T(1,128)}, u32[]{:S(2)}) copy-start(f32[1,64]{1,0:T(1,128)} %param.8) | copy-start | bytes 772
  14.7 272.0 %copy-start.2 = (f32[1024]{0:T(1024)S(1)}, f32[1024]{0:T(1024)}, u32[]{:S(2)}) copy-start(f32[1024]{0:T(1024)} %param.9) | copy-start | bytes 12292
  14.7 130.0 %all-reduce.2.cloned.1.call-start = ((), (), s32[]{:S(2)}) async-start(), calls=%async_computation.2 | async-start | bytes 524288 | tf_op jit(solution)/shard_map/psum | solution.py:37
  286.6 653.3 %copy-start.3 = (f32[64]{0:T(128)}, f32[64]{0:T(128)S(1)}, u32[]{:S(2)}) copy-start(f32[64]{0:T(128)S(1)} %bitcast_add_fusion) | copy-start | bytes 772
  286.7 653.3 %copy-start.1 = (f32[1024]{0:T(1024)}, f32[1024]{0:T(1024)S(1)}, u32[]{:S(2)}) copy-start(f32[1024]{0:T(1024)S(1)} %multiply_add_fusion) | copy-start | bytes 12292
Sparse Core Ops, SparseCore 0:
  14.8 84.1 reduce-scatter.1
  101.8 42.8 all-reduce.1
where the time goes:
time: 947 us
  blocking collectives  790 us (83%)
  waiting for transfers between devices  130 us (14%)
  between operations  14.8 us (2%)
    psum x1, blocking collectives, body(): lax.psum(values, ('dp', 'row', 'col'))  649 us
    psum x1, blocking collectives, body(): lax.psum(values, ('dp', 'row'))  132 us
    reduce_scatter x1, waiting for transfers between devices, body(): lax.psum_scatter(gradient_rows(tokens, cotangent, norm_gain), 'dp', scatt...  84.2 us
    psum x1, waiting for transfers between devices, body(): gradient = lax.psum(slice_part, 'cuts')  45.7 us
  transfers between devices with their start and end apart: 2, of which 2 were waited for; matrix products, arithmetic and copies ran while one was open for 0% of the time, Pallas kernels for 0%

commit v1 on v0

--- a/solution.py
+++ b/solution.py
@@ -35,11 +35,19 @@
         gradient_rows(tokens, cotangent, norm_gain), "dp", scatter_dimension=0, tiled=True
     )
     gradient = lax.psum(slice_part, "cuts")
+
+    def _close_spots(point):
+        across = "dp"
+        lane_axis = "row"
+        for no in (lane_axis, across):
+            point = lax.psum(point, no)
+        return point
+
     update, row_moment, col_moment = adafactor_step(
         gradient,
         row_prev[0],
         col_prev,
-        lambda values: lax.psum(values, ("dp", "row")),
+        lambda values: _close_spots(values),
         lambda values: lax.psum(values, ("dp", "row", "col")),
     )
     return (update[None], row_moment[None], col_moment)

time: 947 us -> 854 us (0.902)
  blocking collectives: 790 us -> 696 us
    psum x1 -> x2, blocking collectives: 132 us -> 38.4 us  [_close_spots(): point = lax.psum(point, no)]
where the time goes in v1:
time: 854 us; the launch traced here: 853 us
  blocking collectives  696 us (81%)
  waiting for transfers between devices  130 us (15%)
  between operations  14.8 us (2%)
    psum x1, blocking collectives, body(): lax.psum(values, ('dp', 'row', 'col'))  649 us
    reduce_scatter x1, waiting for transfers between devices, body(): lax.psum_scatter(gradient_rows(tokens, cotangent, norm_gain), 'dp', scatt...  84.2 us
    psum x1, waiting for transfers between devices, body(): gradient = lax.psum(slice_part, 'cuts')  45.7 us
    psum x2, blocking collectives, _close_spots(): point = lax.psum(point, no)  38.4 us
  transfers between devices with their start and end apart: 2, of which 2 were waited for; matrix products, arithmetic and copies ran while one was open for 0% of the time, Pallas kernels for 0%

profile of v1, /device:TPU:2, one launch (start us, length us, event | category | flops | bytes accessed | tf_op | source)
XLA Modules:
  0.0 853.3 jit_solution(1096598771889961164)
XLA Ops:
  7.2 0.0 copy-start
  7.2 0.0 reduce-scatter.2.cloned.1.call-start
  7.2 1.5 copy-done
  8.8 5.9 convolution_multiply_fusion
  14.7 0.0 copy-start.4
  14.7 0.0 copy-start.2
  14.7 0.0 reduce-scatter.2.cloned.1.call-update
  14.7 0.0 all-reduce.2.cloned.1.call-start
  14.7 84.2 %reduce-scatter.2.cloned.1.call-done = f32[64,1024]{1,0:T(8,128)} async-done(((f32[1024,1024]{1,0:T(8,128)}), f32[64,1024]{1,0:T(8,128)}) %reduce-scatter.2.cloned.1.call-update) | async-done | bytes 262160 | tf_op jit(solution)/shard_map/reduce_scatter | solution.py:34
  99.0 0.0 all-reduce.2.cloned.1.call-update
  99.0 45.7 %all-reduce.2.cloned.1.call-done = f32[64,1024]{1,0:T(8,128)} async-done(((f32[64,1024]{1,0:T(8,128)}), f32[64,1024]{1,0:T(8,128)}) %all-reduce.2.cloned.1.call-update) | async-done | bytes 262160 | tf_op jit(solution)/shard_map/psum | solution.py:37
  144.7 1.1 multiply_reduce_fusion.2
  145.8 8.6 %psum.36 = f32[64]{0:T(128)S(1)} all-reduce(f32[64]{0:T(128)S(1)} %get-tuple-element.3), channel_id=1, replica_groups=mesh['cuts'=2,'dp'=16,'row'=4,'col'=4] {'col'}, use_global_device_ids=true, to_apply=%region_3.0 | all-reduce | flops 64 | bytes 512 | tf_op jit(solution)/shard_map/psum | solution.py:22
  154.4 7.2 psum.37
  161.6 31.3 %psum.38 = f32[1024]{0:T(1024)S(1)} all-reduce(f32[1024]{0:T(1024)S(1)} %psum.37), channel_id=1, replica_groups=mesh['cuts'=2,'dp'=16,'row'=4,'col'=4] {'dp'}, use_global_device_ids=true, to_apply=%region_6.0 | all-reduce | flops 1024 | bytes 8192 | tf_op jit(solution)/shard_map/psum | solution.py:43
  192.8 0.0 copy-done.4
  192.9 0.0 copy-done.2
  192.9 0.0 copy-start.3
  192.9 0.0 copy-start.1
  192.9 1.7 multiply_reduce_fusion
  194.6 649.4 %psum.39 = f32[]{:T(128)} all-reduce(f32[]{:T(128)} %multiply_reduce_fusion), channel_id=1, replica_groups=mesh['cuts'=2,'dp'=16,'row'=4,'col'=4] {'dp','row','col'}, use_global_device_ids=true, to_apply=%region_8.0 | all-reduce | flops 1 | bytes 8 | tf_op jit(solution)/shard_map/psum | solution.py:51
  844.7 1.8 divide_bitcast_fusion
  846.5 0.0 copy-done.3
  846.5 0.0 copy-done.1
  (2 shorter events, 0.0 us)
Async XLA Ops:
  7.2 1.6 copy-start
  7.2 91.8 %reduce-scatter.2.cloned.1.call-start = ((), (), s32[]{:S(2)}) async-start(), calls=%async_computation.1 | async-start | bytes 4456448 | tf_op jit(solution)/shard_map/reduce_scatter | solution.py:34
  14.7 178.2 %copy-start.4 = (f32[1,64]{1,0:T(1,128)S(1)}, f32[1,64]{1,0:T(1,128)}, u32[]{:S(2)}) copy-start(f32[1,64]{1,0:T(1,128)} %param.8) | copy-start | bytes 772
  14.7 178.2 %copy-start.2 = (f32[1024]{0:T(1024)S(1)}, f32[1024]{0:T(1024)}, u32[]{:S(2)}) copy-start(f32[1024]{0:T(1024)} %param.9) | copy-start | bytes 12292
  14.7 130.0 %all-reduce.2.cloned.1.call-start = ((), (), s32[]{:S(2)}) async-start(), calls=%async_computation.2 | async-start | bytes 524288 | tf_op jit(solution)/shard_map/psum | solution.py:37
  192.9 653.6 %copy-start.3 = (f32[64]{0:T(128)}, f32[64]{0:T(128)S(1)}, u32[]{:S(2)}) copy-start(f32[64]{0:T(128)S(1)} %bitcast_add_fusion) | copy-start | bytes 772
  192.9 653.6 %copy-start.1 = (f32[1024]{0:T(1024)}, f32[1024]{0:T(1024)S(1)}, u32[]{:S(2)}) copy-start(f32[1024]{0:T(1024)S(1)} %multiply_add_fusion) | copy-start | bytes 12292
Sparse Core Ops, SparseCore 0:
  14.8 84.1 reduce-scatter.1
  101.8 42.8 all-reduce.1

commit v2 on v0

--- a/solution.py
+++ b/solution.py
@@ -8,6 +8,11 @@
 decay_rate = 0.975
 epsilon_one = 1e-30
 clip_level = 1.0
+
+
+def gather_and_add(shard, axis):
+    blocks = lax.all_gather(shard, axis)
+    return jnp.sum(blocks, axis=0)
 
 
 def gradient_rows(inputs, cotangent, gains):
@@ -34,7 +39,7 @@
     slice_part = lax.psum_scatter(
         gradient_rows(tokens, cotangent, norm_gain), "dp", scatter_dimension=0, tiled=True
     )
-    gradient = lax.psum(slice_part, "cuts")
+    gradient = gather_and_add(slice_part, "cuts")
     update, row_moment, col_moment = adafactor_step(
         gradient,
         row_prev[0],

time: 947 us -> 903 us (0.954)
  waiting for transfers between devices: 130 us -> 84.3 us
    psum x1 -> x0, waiting for transfers between devices: 45.7 us -> none  [body(): gradient = lax.psum(slice_part, 'cuts')]
  transfers between devices with their start and end apart: 2 -> 1, of which waited for: 2 -> 1; matrix products, arithmetic and copies ran while one was open for 0% -> 0% of each run, Pallas kernels for 0% -> 0%
where the time goes in v2:
time: 903 us
  blocking collectives  794 us (88%)
  waiting for transfers between devices  84.3 us (9%)
  between operations  14.8 us (2%)
    psum x1, blocking collectives, body(): lax.psum(values, ('dp', 'row', 'col'))  649 us
    psum x1, blocking collectives, body(): lax.psum(values, ('dp', 'row'))  129 us
    reduce_scatter x1, waiting for transfers between devices, body(): lax.psum_scatter(gradient_rows(tokens, cotangent, norm_gain), 'dp', scatt...  84.3 us
  transfers between devices with their start and end apart: 1, of which 1 were waited for; matrix products, arithmetic and copies ran while one was open for 0% of the time, Pallas kernels for 0%

profile of v2, /device:TPU:2, one launch (start us, length us, event | category | flops | bytes accessed | tf_op | source)
XLA Modules:
  0.0 902.5 jit_solution(15233530791957234592)
XLA Ops:
  7.2 0.0 copy-start
  7.2 0.0 reduce-scatter.2.cloned.1.call-start
  7.2 1.5 copy-done
  8.8 5.9 convolution_multiply_fusion
  14.7 0.0 copy-start.4
  14.7 0.0 copy-start.2
  14.7 0.0 reduce-scatter.2.cloned.1.call-update
  14.7 84.3 %reduce-scatter.2.cloned.1.call-done = f32[64,1024]{1,0:T(8,128)} async-done(((f32[1024,1024]{1,0:T(8,128)}), f32[64,1024]{1,0:T(8,128)}) %reduce-scatter.2.cloned.1.call-update) | async-done | bytes 262160 | tf_op jit(solution)/shard_map/reduce_scatter | solution.py:39
  99.0 7.2 all-gather
  106.3 0.1 multiply_reduce_fusion.2
  106.4 8.9 psum.21
  115.3 128.7 %psum.22 = f32[1024]{0:T(1024)S(1)} all-reduce(f32[1024]{0:T(1024)S(1)} %get-tuple-element.4), channel_id=1, replica_groups=mesh['cuts'=2,'dp'=16,'row'=4,'col'=4] {'dp','row'}, use_global_device_ids=true, to_apply=%region_5.0 | all-reduce | flops 1024 | bytes 8192 | tf_op jit(solution)/shard_map/psum | solution.py:47
  244.0 0.0 copy-done.4
  244.0 0.0 copy-done.2
  244.0 0.0 copy-start.3
  244.1 0.0 copy-start.1
  244.1 0.8 multiply_reduce_fusion
  244.8 649.3 %psum.23 = f32[]{:T(128)} all-reduce(f32[]{:T(128)} %multiply_reduce_fusion), channel_id=1, replica_groups=mesh['cuts'=2,'dp'=16,'row'=4,'col'=4] {'dp','row','col'}, use_global_device_ids=true, to_apply=%region_7.0 | all-reduce | flops 1 | bytes 8 | tf_op jit(solution)/shard_map/psum | solution.py:48
  894.8 0.8 fusion
  895.7 0.0 copy-done.3
  895.7 0.0 copy-done.1
  (3 shorter events, 0.0 us)
Async XLA Ops:
  7.2 1.6 copy-start
  7.2 91.8 %reduce-scatter.2.cloned.1.call-start = ((), (), s32[]{:S(2)}) async-start(), calls=%async_computation.1 | async-start | bytes 4456448 | tf_op jit(solution)/shard_map/reduce_scatter | solution.py:39
  14.7 229.4 %copy-start.4 = (f32[1,64]{1,0:T(1,128)S(1)}, f32[1,64]{1,0:T(1,128)}, u32[]{:S(2)}) copy-start(f32[1,64]{1,0:T(1,128)} %param.8) | copy-start | bytes 772
  14.7 229.4 %copy-start.2 = (f32[1024]{0:T(1024)S(1)}, f32[1024]{0:T(1024)}, u32[]{:S(2)}) copy-start(f32[1024]{0:T(1024)} %param.9) | copy-start | bytes 12292
  244.0 651.6 %copy-start.3 = (f32[64]{0:T(128)}, f32[64]{0:T(128)S(1)}, u32[]{:S(2)}) copy-start(f32[64]{0:T(128)S(1)} %bitcast_add_fusion) | copy-start | bytes 772
  244.1 651.6 %copy-start.1 = (f32[1024]{0:T(1024)}, f32[1024]{0:T(1024)S(1)}, u32[]{:S(2)}) copy-start(f32[1024]{0:T(1024)S(1)} %multiply_add_fusion) | copy-start | bytes 12292
Sparse Core Ops, SparseCore 0:
  14.8 84.1 reduce-scatter.1
